TPU v7x, 32 devices: a whole 2x2x4 slice. The times are simulated.
32 devices in a mesh: sub: 2 (over y), row: 8 (over z, x), col: 2 (over core).
Axes of the slice: x: 2, y: 2, z: 4, core: 2. Of those that a mesh axis runs over, the one named last changes fastest.
Arguments:
- child_pivot: float32 [2, 1024, 1024], P('sub', 'row'), as said below
- child_border: float32 [2, 4096, 1024], P('sub', 'row'), as said below
- child_update: float32 [2, 4096, 4096], P('sub', 'row', 'col'), as said below
- parent_front: float32 [16384, 16384], P('row', ('sub', 'col')), as said below
- tile_map: int32 [2, 32], replicated, may hold values from -1 to 127, as said below
Outputs:
- schur_block: float32 [16384, 16384], P('row', ('sub', 'col'))
- panel_rows: float32 [16384, 256], P('row')
Inputs may be any that keep to these rules, and one draw needn't show every extreme that they name: For each child s the matrix [[child_pivot[s], child_border[s]^T], [child_border[s], child_update[s]]] is symmetric positive definite; child_pivot[s] and child_update[s] are symmetric. `child_border`: see child_pivot: the border of a symmetric positive definite child front. `child_update`: see child_pivot: the trailing block of a symmetric positive definite child front. `parent_front`: symmetric positive definite. tile_map[s, t] is the parent tile that receives tile t of child s, or -1 where t lies beyond child s's front; the -1 entries of a child come after its live ones, every child has 16 live tiles or more, some child has all 32 live and some exactly 16; the live entries of one child are distinct; the child tiles t with t // 4 == i map into parent tiles i * 16 to (i + 1) * 16 - 1.
All inputs are finite; a program needn't handle non-finite values.
Results may differ from a plain program's by a relative error of at most 0.0001.
Values sent between devices are 32-bit elements; how exact they have to be, the bound alone decides.
A program may use at most 192 MiB of HBM per device.

v0:
```python
import jax
import jax.numpy as jnp
from jax import lax
from jax.sharding import PartitionSpec as P

PANEL = 256
TILE = 128


highest = lax.Precision.HIGHEST


def from_root(block, axis, owner):
    block = jnp.where(lax.axis_index(axis) == owner, block, jnp.zeros_like(block))
    return lax.psum(block, axis)


def solve_rows(lower_tri, right_rows):
    return jax.scipy.linalg.solve_triangular(lower_tri, right_rows.T, lower=True).T


def onehot_tiles(tile_ids, first_tile, width):
    local_ids = tile_ids - first_tile
    return (local_ids[:, :, None] == jnp.arange(width, dtype=jnp.int32)[None, None, :]).astype(
        jnp.float32
    )


def on_device(child_pivot, child_border, child_update, parent_front, tile_map):
    sub_count = lax.axis_size("sub")
    column_count = lax.axis_size("col")
    row_index = lax.axis_index("row")
    column_index = lax.axis_index("col")
    my_group = lax.axis_index("sub") * column_count + column_index
    local_rows = child_update.shape[1]
    half_cols = child_update.shape[2]
    group_width = half_cols // sub_count
    pivot_full = lax.all_gather(child_pivot[0], "row", axis=0, tiled=True)
    border_local = child_border[0]
    all_border = lax.all_gather(border_local, "row", axis=0, tiled=True)
    lower_tri = jnp.linalg.cholesky(pivot_full)
    own_factor = solve_rows(lower_tri, border_local)
    far_border = lax.dynamic_slice_in_dim(all_border, column_index * half_cols, half_cols, 0)
    far_factor = solve_rows(lower_tri, far_border)
    contrib = child_update[0] - jnp.dot(
        own_factor, far_factor.T, precision=highest, preferred_element_type=jnp.float32
    )
    padded = jnp.zeros((local_rows, half_cols * column_count), jnp.float32)
    padded = lax.dynamic_update_slice_in_dim(padded, contrib, column_index * half_cols, 1)
    received = lax.all_to_all(padded, ("sub", "col"), split_axis=1, concat_axis=0, tiled=True)
    received = received.reshape(sub_count, column_count, local_rows, group_width)
    arrived = lax.dynamic_index_in_dim(received, my_group // sub_count, 1, keepdims=False)
    row_tiles = local_rows // TILE
    group_tiles = group_width // TILE
    parent_rows = parent_front.shape[0]
    parent_cols = parent_front.shape[1]
    tile_rows = lax.dynamic_slice_in_dim(tile_map, row_index * row_tiles, row_tiles, 1)
    tile_cols = lax.dynamic_slice_in_dim(tile_map, my_group * group_tiles, group_tiles, 1)
    row_onehot = onehot_tiles(tile_rows, row_index * (parent_rows // TILE), parent_rows // TILE)
    column_onehot = onehot_tiles(tile_cols, my_group * (parent_cols // TILE), parent_cols // TILE)
    blocks = arrived.reshape(sub_count, row_tiles, TILE, group_tiles, TILE)
    placed = jnp.einsum("skb,sixkz->sixbz", column_onehot, blocks, precision=highest)
    assembled = jnp.einsum("sia,sixbz->axbz", row_onehot, placed, precision=highest)
    parent = parent_front + assembled.reshape(parent_rows, parent_cols)
    group_zero = from_root(parent[:, :PANEL], ("sub", "col"), 0)
    top_block = from_root(group_zero[:PANEL], "row", 0)
    top_lower = jnp.linalg.cholesky(top_block)
    panel_rows = solve_rows(top_lower, group_zero)
    per_group = parent_cols // parent_rows
    pieces = []
    for member in range(per_group):
        pieces.append(from_root(panel_rows, "row", my_group * per_group + member))
    column_panel = jnp.concatenate(pieces, axis=0)
    schur_block = parent - jnp.dot(
        panel_rows, column_panel.T, precision=highest, preferred_element_type=jnp.float32
    )
    return (schur_block, panel_rows)


def solution(mesh):
    placed = (
        P("sub", "row", None),
        P("sub", "row", None),
        P("sub", "row", "col"),
        P("row", ("sub", "col")),
        P(),
    )
    return jax.shard_map(
        on_device,
        mesh=mesh,
        in_specs=placed,
        out_specs=(P("row", ("sub", "col")), P("row", None)),
        check_vma=False,
    )
```

profile of v0, /device:TPU:0, one launch (start us, length us, event | category | flops | bytes accessed | tf_op | source)
XLA Modules:
  0.0 1166.0 jit_solution(13474759776697304241)
XLA Ops:
  12.0 76.4 %all-gather.5.cloned.1.call-done = f32[1,1024,1024]{1,2,0:T(8,128)} async-done(((f32[1,128,1024]{1,2,0:T(8,128)}), f32[1,1024,1024]{1,2,0:T(8,128)}) %all-gather.5.cloned.1.call-update) | async-done | bytes 4194320 | tf_op jit(solution)/shard_map/all_gather | solution.py:38
  101.1 11.7 %cholesky.249 = f32[128,128]{1,0:T(8,128)S(1)} custom-call(f32[128,128]{1,0:T(8,128)S(1)} %cholesky.650), custom_call_target="Cholesky" | custom-call | tf_op jit(solution)/shard_map/jit(cholesky)/cholesky | solution.py:41
  112.8 9.8 custom-call.74
  129.1 12.0 %cholesky.272 = f32[128,128]{1,0:T(8,128)S(1)} custom-call(f32[128,128]{1,0:T(8,128)S(1)} %cholesky.654), custom_call_target="Cholesky" | custom-call | tf_op jit(solution)/shard_map/jit(cholesky)/cholesky | solution.py:41
  141.8 9.8 custom-call.75
  154.9 11.7 %cholesky.299 = f32[128,128]{1,0:T(8,128)S(1)} custom-call(f32[128,128]{1,0:T(8,128)S(1)} %cholesky.659), custom_call_target="Cholesky" | custom-call | tf_op jit(solution)/shard_map/jit(cholesky)/cholesky | solution.py:41
  167.2 9.8 custom-call.76
  180.7 11.9 %cholesky.539 = f32[128,128]{1,0:T(8,128)S(1)} custom-call(f32[128,128]{1,0:T(8,128)S(1)} %cholesky.664), custom_call_target="Cholesky" | custom-call | tf_op jit(solution)/shard_map/jit(cholesky)/cholesky | solution.py:41
  193.2 9.8 custom-call.77
  206.5 11.7 %cholesky.558 = f32[128,128]{1,0:T(8,128)S(1)} custom-call(f32[128,128]{1,0:T(8,128)S(1)} %cholesky.669), custom_call_target="Cholesky" | custom-call | tf_op jit(solution)/shard_map/jit(cholesky)/cholesky | solution.py:41
  218.8 10.0 custom-call.78
  232.1 11.7 %cholesky.578 = f32[128,128]{1,0:T(8,128)S(1)} custom-call(f32[128,128]{1,0:T(8,128)S(1)} %cholesky.674), custom_call_target="Cholesky" | custom-call | tf_op jit(solution)/shard_map/jit(cholesky)/cholesky | solution.py:41
  257.2 11.7 %cholesky.598 = f32[128,128]{1,0:T(8,128)S(1)} custom-call(f32[128,128]{1,0:T(8,128)S(1)} %cholesky.679), custom_call_target="Cholesky" | custom-call | tf_op jit(solution)/shard_map/jit(cholesky)/cholesky | solution.py:41
  269.6 9.8 custom-call.83
  282.0 11.7 %cholesky.612 = f32[128,128]{1,0:T(8,128)S(1)} custom-call(f32[128,128]{1,0:T(8,128)S(1)} %convolution_subtract_fusion.21), custom_call_target="Cholesky" | custom-call | tf_op jit(solution)/shard_map/jit(cholesky)/cholesky | solution.py:41
  308.5 22.9 %while.2 = (s32[]{:T(128)}, f32[1024,1024]{1,0:T(8,128)}, s32[8,2]{0,1:T(2,128)S(1)}, f32[8,128,128]{2,1,0:T(8,128)S(1)}, s32[]{:T(128)}) while((s32[]{:T(128)}, f32[1024,1024]{1,0:T(8,128)}, s32[8,2]{0,1:T(2,128)S(1)}, f32[8,128,128]{2,1,0:T(8,128)S(1)}, s32[]{:T(128)}) %tuple.107), condition=%wide.while_cond, body=%wide.while_body.sunk | while | flops 2 | bytes 131181 | solution.py:19
  331.4 78.8 %custom-call.80 = f32[8,128,128]{1,2,0:T(8,128)S(1)} custom-call(f32[8,128,128]{2,1,0:T(8,128)S(1)} %get-tuple-element.10), custom_call_target="InvertDiagBlocksLowerTriangular" | custom-call | tf_op jit(solution)/shard_map/jit(_solve_triangular)/triangular_solve | solution.py:19
  489.1 17.0 %bitcast_subtract_fusion = f32[512,2048]{1,0:T(8,128)} fusion(f32[1,512,2048]{2,1,0:T(8,128)S(1)} %copy-done.4, f32[1024,512]{1,0:T(8,128)} %convolution_dynamic-update-slice_fusion.3, f32[1024,2048]{1,0:T(8,128)S(1)} %convolution_dynamic-update-slice_fusion), kind=kOutput, calls=%fused_computation.21 | convolution fusion | flops 12885950464 | bytes 18874368 | tf_op jit(solution)/shard_map/dot_general | solution.py:45
  532.8 33.6 %copy.41 = f32[2048,4096]{0,1:T(8,128)} copy(f32[2048,4096]{1,0:T(8,128)} %param.10) | data formatting | bytes 67108864 | tf_op args[3]
  566.6 59.3 %all-to-all-done = f32[512,4,1024]{2,0,1:T(8,128)} async-done(((f32[512,4,1024]{2,0,1:T(8,128)}), f32[512,4,1024]{2,0,1:T(8,128)}, u32[]{:S(2)}, u32[]{:S(2)}) %all-to-all-start) | async-done | bytes 8388640 | tf_op jit(solution)/shard_map/all_to_all | solution.py:50
  639.2 15.4 %copy.52 = f32[2,4,128,32,128]{2,1,0,4,3:T(4,128)} copy(f32[2,4,128,32,128]{4,3,2,1,0:T(8,128)} %convolution_bitcast_fusion) | data formatting | bytes 33554432 | tf_op jit(solution)/shard_map/skb,sixkz->sixbz/transpose | solution.py:62
  654.5 24.5 %fusion.112 = f32[16,128,32,128,1]{1,0,4,3,2:T(8,128)} fusion(f32[2,4,128,32,128]{2,1,0,4,3:T(4,128)} %copy.52, pred[2,4,16,1,1]{2,1,0,4,3:T(4,128)(4,1)S(1)} %fusion.160), kind=kOutput, calls=%fused_computation.238 | convolution fusion | flops 805306368 | bytes 50331776 | tf_op jit(solution)/shard_map/sia,sixbz->axbz/dot_general | solution.py:63
  679.0 37.2 %bitcast_add_fusion = f32[2048,4096]{0,1:T(8,128)} fusion(f32[2048,4096]{0,1:T(8,128)} %copy.41, f32[512,8,16,128]{3,2,1,0:T(8,128)} %bitcast.227), kind=kLoop, calls=%fused_computation.4 | loop fusion | flops 8388608 | bytes 100663296 | tf_op jit(solution)/shard_map/add | solution.py:64
  719.4 48.4 %all-reduce.7.cloned.1.call-done = f32[2048,256]{0,1:T(8,128)} async-done(((f32[2048,256]{0,1:T(8,128)}), f32[2048,256]{0,1:T(8,128)}) %all-reduce.7.cloned.1.call-update) | async-done | bytes 2097168 | tf_op jit(solution)/shard_map/psum | solution.py:15
  770.1 72.5 %all-reduce.9.cloned.1.call-done = f32[256,256]{0,1:T(8,128)} async-done(((f32[256,256]{0,1:T(8,128)}), f32[256,256]{0,1:T(8,128)}) %all-reduce.9.cloned.1.call-update) | async-done | bytes 262160 | tf_op jit(solution)/shard_map/psum | solution.py:15
  844.7 11.7 %cholesky.626 = f32[128,128]{1,0:T(8,128)S(1)} custom-call(f32[128,128]{1,0:T(8,128)S(1)} %cholesky.683), custom_call_target="Cholesky" | custom-call | tf_op jit(solution)/shard_map/jit(cholesky)/cholesky | solution.py:67
  856.6 9.8 custom-call.84
  867.0 11.7 %cholesky.635 = f32[128,128]{1,0:T(8,128)S(1)} custom-call(f32[128,128]{1,0:T(8,128)S(1)} %convolution_subtract_fusion.20), custom_call_target="Cholesky" | custom-call | tf_op jit(solution)/shard_map/jit(cholesky)/cholesky | solution.py:67
  885.8 19.7 %custom-call.81 = f32[2,128,128]{1,2,0:T(8,128)S(1)} custom-call(f32[2,128,128]{2,1,0:T(8,128)S(1)} %get-tuple-element.18), custom_call_target="InvertDiagBlocksLowerTriangular" | custom-call | tf_op jit(solution)/shard_map/jit(_solve_triangular)/triangular_solve | solution.py:19
  915.5 151.7 %all-reduce.11.cloned.1.call-done = (f32[2048,256]{0,1:T(8,128)}, f32[2048,256]{0,1:T(8,128)}) async-done(((f32[2048,256]{0,1:T(8,128)}, f32[2048,256]{0,1:T(8,128)}), (f32[2048,256]{0,1:T(8,128)}, f32[2048,256]{0,1:T(8,128)})) %all-reduce.11.cloned.1.call-update) | async-done | bytes 4194320 | tf_op jit(solution)/shard_map/psum | solution.py:15
  1067.3 60.9 %convolution_subtract_fusion = f32[2048,4096]{0,1:T(8,128)} fusion(f32[2048,4096]{0,1:T(8,128)} %bitcast_add_fusion, f32[2048,256]{0,1:T(8,128)} %get-tuple-element.53, f32[2048,256]{0,1:T(8,128)} %get-tuple-element.54, f32[128,2048]{1,0:T(8,128)S(1)} %fusion.82, f32[128,2048]{1,0:T(8,128)S(1)} %fusion.29), kind=kOutput, calls=%fused_computation.5 | convolution fusion | flops 25779765248 | bytes 73400320 | tf_op jit(solution)/shard_map/dot_general | solution.py:74
  1128.2 31.1 %copy.47 = f32[2048,4096]{1,0:T(8,128)} copy(f32[2048,4096]{0,1:T(8,128)} %convolution_subtract_fusion) | data formatting | bytes 67108864
  (179 shorter events, 236.7 us)
Async XLA Ops:
  7.2 3.0 copy-start.2
  7.2 81.2 %all-gather.5.cloned.1.call-start = ((), (), s32[]{:S(2)}) async-start(), calls=%async_computation.3 | async-start | bytes 4718592 | tf_op jit(solution)/shard_map/all_gather | solution.py:38
  9.4 422.0 %all-gather.7.cloned.1.call-start = ((), (), s32[]{:S(2)}) async-start(), calls=%async_computation.4 | async-start | bytes 18874368 | tf_op jit(solution)/shard_map/all_gather | solution.py:40
  99.0 2.0 copy-start.1
  303.5 106.7 %copy-start.3 = (f32[1,512,1024]{1,2,0:T(8,128)S(1)}, f32[1,512,1024]{1,2,0:T(8,128)}, u32[]{:S(2)}) copy-start(f32[1,512,1024]{1,2,0:T(8,128)} %copy.34) | copy-start | bytes 6291460
  449.2 6.4 slice-start
  451.9 3.8 slice-start.1
  482.4 6.6 copy-start.4
  511.4 4.5 copy-start
  527.0 98.8 %all-to-all-start = ((f32[512,4,1024]{2,0,1:T(8,128)}), f32[512,4,1024]{2,0,1:T(8,128)}, u32[]{:S(2)}, u32[]{:S(2)}) async-start(f32[512,4,1024]{2,0,1:T(8,128)} %copy.37), calls=%async_computation | async-start | bytes 16777216 | tf_op jit(solution)/shard_map/all_to_all | solution.py:50
  532.7 235.1 %all-reduce.7.cloned.1.call-start = ((), (), s32[]{:S(2)}) async-start(), calls=%async_computation.1 | async-start | bytes 4194304 | tf_op jit(solution)/shard_map/psum | solution.py:15
  532.8 33.6 %copy-start.6 = (s32[2,32]{1,0:T(2,128)S(1)}, s32[2,32]{1,0:T(2,128)}, u32[]{:S(2)}) copy-start(s32[2,32]{1,0:T(2,128)} %param.11) | copy-start | bytes 772
  719.4 123.2 %all-reduce.9.cloned.1.call-start = ((), (), s32[]{:S(2)}) async-start(), calls=%async_computation.2 | async-start | bytes 524288 | tf_op jit(solution)/shard_map/psum | solution.py:15
  767.8 137.7 %copy-start.5 = (f32[2048,256]{0,1:T(8,128)S(1)}, f32[2048,256]{0,1:T(8,128)}, u32[]{:S(2)}) copy-start(f32[2048,256]{0,1:T(8,128)} %all-reduce.7.cloned.1.call-done) | copy-start | bytes 6291460
  769.6 297.6 %all-reduce.11.cloned.1.call-start = ((), (), s32[]{:S(2)}) async-start(), calls=%async_computation.5 | async-start | bytes 8388608 | tf_op jit(solution)/shard_map/psum | solution.py:15
Sparse Core Ops, SparseCore 0:
  10.6 77.7 all-gather.4
  90.5 225.9 all-gather.6
  719.5 48.2 all-reduce.6
  772.0 70.6 all-reduce.8
  911.3 155.9 all-reduce.10
where the time goes:
time: 1180 us; the launch traced here: 1170 us
  waiting for transfers between devices  409 us (35%)
  other arithmetic  363 us (31%)
  matrix products  200 us (17%)
  local copies, waits for them, and re-layouts  167 us (14%)
  between operations  20.6 us (2%)
    psum x3, waiting for transfers between devices, from_root(): return lax.psum(block, axis)  273 us
    another operation x30, other arithmetic, on_device(): lower_tri = jnp.linalg.cholesky(pivot_full)  172 us
    another operation x6, other arithmetic, solve_rows(): jax.scipy.linalg.solve_triangular(lower_tri, right_rows.T, lower=True)  103 us
    all_gather x1, waiting for transfers between devices, on_device(): pivot_full = lax.all_gather(child_pivot[0], 'row', axis=0, tiled=True)  76.4 us
    unnamed x24, local copies, waits for them, and re-layouts  74.6 us
    another operation x33, matrix products, solve_rows(): jax.scipy.linalg.solve_triangular(lower_tri, right_rows.T, lower=True)  64 us
    dot_general x1, matrix products, on_device(): jnp.dot(panel_rows, column_panel.T, precision=highest, preferred_element_...  60.9 us
    all_to_all x1, waiting for transfers between devices, on_device(): lax.all_to_all(padded, ('sub', 'col'), split_axis=1, concat_axis=0, tiled...  59.3 us
  transfers between devices with their start and end apart: 6, of which 5 were waited for; matrix products, arithmetic and copies ran while one was open for 32% of the time, Pallas kernels for 0%

commit v1 on v0

v1 whole, which is shorter than its diff:
```python
import functools

import jax
import jax.numpy as jnp
from jax import lax
from jax.experimental import pallas as pl
from jax.experimental.pallas import tpu as pltpu
from jax.sharding import PartitionSpec as P

PANEL = 256
TILE = 128
STRIP = 32
SLAB = 256

high = lax.Precision.HIGH
highest = lax.Precision.HIGHEST
BY_COLUMNS = (((1,), (1,)), ((), ()))


def mm(left, right):
    return jnp.dot(left, right, precision=highest, preferred_element_type=jnp.float32)


def times_transposed(left, right):
    return lax.dot_general(
        left, right, BY_COLUMNS, precision=high, preferred_element_type=jnp.float32
    )


def invert_tile(block):
    lane = lax.broadcasted_iota(jnp.int32, (STRIP, TILE), 1)
    row = lax.broadcasted_iota(jnp.int32, (STRIP, TILE), 0)
    first = 0
    rest = block
    done = []
    while first < TILE:
        strip = rest[:STRIP]
        for step in range(STRIP):
            pivot = first + step
            scale = lax.rsqrt(strip[step : step + 1, pivot : pivot + 1])
            column = jnp.broadcast_to(strip[:, pivot : pivot + 1], (STRIP, TILE))
            at_pivot = lane == pivot
            scaled = jnp.where(at_pivot[:1], 1.0, strip[step : step + 1]) * scale
            below = jnp.where(row > step, column, 0.0) * scale
            kept = jnp.where(at_pivot, 0.0, strip) - below * scaled
            strip = jnp.where(row == step, jnp.broadcast_to(scaled, (STRIP, TILE)), kept)
        done.append(strip)
        first += STRIP
        if first < TILE:
            rest = rest[STRIP:]
            columns = lax.broadcasted_iota(jnp.int32, rest.shape, 1)
            cleared = (columns >= first - STRIP) & (columns < first)
            rest = jnp.where(cleared, 0.0, rest) - mm(strip.T[first:], strip)
    whole = jnp.concatenate(done, axis=0)
    lane = lax.broadcasted_iota(jnp.int32, (TILE, TILE), 1)
    row = lax.broadcasted_iota(jnp.int32, (TILE, TILE), 0)
    return jnp.where(lane > row, 0.0, whole)


def invert_factor(work, strip):
    order = work.shape[0]
    tiles = order // TILE

    def tile_at(index):
        return pl.ds(pl.multiple_of(index * TILE, TILE), TILE)

    def eliminate(k, carry):
        here = tile_at(k)
        corner = invert_tile(work[here, here])
        strip[...] = mm(corner, work[here, :])
        strip[:, here] = corner

        def update(i, inner):
            there = tile_at(i)
            work[there, here] = jnp.zeros((TILE, TILE), jnp.float32)
            work[there, :] = work[there, :] - mm(strip[:, there].T, strip[...])
            return inner

        lax.fori_loop(k + 1, tiles, update, 0)
        columns = lax.broadcasted_iota(jnp.int32, (TILE, order), 1)
        work[here, :] = jnp.where(columns < (k + 1) * TILE, strip[...], 0.0)
        return carry

    lax.fori_loop(0, tiles, eliminate, 0)


def pivot_kernel(pivot_ref, inverse_ref, strip):
    inverse_ref[...] = pivot_ref[...]
    invert_factor(inverse_ref, strip)


def whole_block(shape):
    return pl.BlockSpec(shape, lambda *_: (0,) * len(shape))


def invert_pivot(pivot):
    order = pivot.shape[0]
    return pl.pallas_call(
        pivot_kernel,
        out_shape=jax.ShapeDtypeStruct((order, order), jnp.float32),
        in_specs=[pl.BlockSpec(memory_space=pltpu.VMEM)],
        out_specs=pl.BlockSpec(memory_space=pltpu.VMEM),
        scratch_shapes=[pltpu.VMEM((TILE, order), jnp.float32)],
        compiler_params=pltpu.CompilerParams(vmem_limit_bytes=40 * 2**20),
        cost_estimate=pl.CostEstimate(
            flops=40 * order**3, bytes_accessed=8 * order**2, transcendentals=order
        ),
        name="invert_pivot",
    )(pivot)


def add_row_tiles(map_ref, first, tiles, limit, sent_ref, target):
    for child in range(sent_ref.shape[0]):
        for r in range(tiles):
            place = map_ref[child, first + r]

            @pl.when((place >= 0) & (lax.rem(jnp.maximum(place, 0), limit[0]) < limit[1]))
            def _():
                spot = lax.rem(place, limit[0])
                rows = pl.ds(pl.multiple_of(spot * TILE, TILE), TILE)
                target[rows, :] += sent_ref[child, r * TILE : (r + 1) * TILE, :]


def top_kernel(block_tiles, map_ref, front_ref, sent_ref, inverse_ref, strip):
    inverse_ref[...] = front_ref[...]
    tiles = sent_ref.shape[1] // TILE
    add_row_tiles(map_ref, 0, tiles, (block_tiles, PANEL // TILE), sent_ref, inverse_ref)
    invert_factor(inverse_ref, strip)


def invert_top(tile_map, front_panel, sent, block_rows, child_rows):
    children = sent.shape[0]
    return pl.pallas_call(
        functools.partial(top_kernel, block_rows // TILE),
        out_shape=jax.ShapeDtypeStruct((PANEL, PANEL), jnp.float32),
        grid_spec=pltpu.PrefetchScalarGridSpec(
            num_scalar_prefetch=1,
            grid=(1,),
            in_specs=[
                whole_block((PANEL, PANEL)),
                whole_block((children, child_rows, PANEL)),
            ],
            out_specs=whole_block((PANEL, PANEL)),
            scratch_shapes=[pltpu.VMEM((TILE, PANEL), jnp.float32)],
        ),
        compiler_params=pltpu.CompilerParams(vmem_limit_bytes=32 * 2**20),
        name="invert_top",
    )(tile_map, front_panel, sent)


def panel_kernel(block_tiles, ids_ref, map_ref, front_ref, sent_ref, inverse_ref, out_ref, held):
    held[...] = front_ref[...]
    tiles = sent_ref.shape[1] // TILE
    first = ids_ref[pl.program_id(0)] * tiles
    add_row_tiles(map_ref, first, tiles, (block_tiles, block_tiles), sent_ref, held)
    out_ref[...] = lax.dot_general(
        held[...], inverse_ref[...], BY_COLUMNS, precision=highest,
        preferred_element_type=jnp.float32,
    )


def factor_panel(block_ids, tile_map, front_panel, sent, inverse, block_rows, child_rows):
    children = sent.shape[0]
    count = block_ids.shape[0]
    return pl.pallas_call(
        functools.partial(panel_kernel, block_rows // TILE),
        out_shape=jax.ShapeDtypeStruct((count * block_rows, PANEL), jnp.float32),
        grid_spec=pltpu.PrefetchScalarGridSpec(
            num_scalar_prefetch=2,
            grid=(count,),
            in_specs=[
                pl.BlockSpec((block_rows, PANEL), lambda i, ids, _: (ids[i], 0)),
                pl.BlockSpec((children, child_rows, PANEL), lambda i, ids, _: (0, ids[i], 0)),
                whole_block((PANEL, PANEL)),
            ],
            out_specs=pl.BlockSpec((block_rows, PANEL), lambda i, ids, _: (i, 0)),
            scratch_shapes=[pltpu.VMEM((block_rows, PANEL), jnp.float32)],
        ),
        compiler_params=pltpu.CompilerParams(vmem_limit_bytes=48 * 2**20),
        name="factor_panel",
    )(block_ids, tile_map, front_panel, sent, inverse)


def two_parts(value):
    upper = value.astype(jnp.bfloat16)
    return upper, (value - upper.astype(jnp.float32)).astype(jnp.bfloat16)


def schur_kernel(rows_ref, cols_ref, parent_ref, panel_ref, *rest):
    *arrived, out_ref, split = rest
    step = pl.program_id(0)
    slab, width = out_ref.shape
    chunk = min(width, 1024)
    offset = panel_ref.shape[0] - width

    @pl.when(step == 0)
    def _():
        def cut(i, carry):
            source = pl.ds(pl.multiple_of(offset + i * SLAB, SLAB), SLAB)
            upper, lower = two_parts(panel_ref[source, :])
            target = pl.ds(pl.multiple_of(i * SLAB, SLAB), SLAB)
            split[target, 0:PANEL] = upper
            split[target, PANEL : 2 * PANEL] = lower
            split[target, 2 * PANEL : 3 * PANEL] = upper
            return carry

        lax.fori_loop(0, width // SLAB, cut, 0)

    own = panel_ref[pl.ds(pl.multiple_of(step * slab, slab), slab), :]
    upper, lower = two_parts(own)
    left = jnp.concatenate([upper, upper, lower], axis=1)
    for start in range(0, width, chunk):
        product = lax.dot_general(
            left, split[start : start + chunk, :], BY_COLUMNS, preferred_element_type=jnp.float32
        )
        out_ref[:, start : start + chunk] = parent_ref[:, start : start + chunk] - product

    slab_tiles = slab // TILE
    for index, block in enumerate(arrived):
        for r in range(block.shape[0] // TILE):
            place = rows_ref[index, r]
            local = place - step * slab_tiles

            @pl.when((place >= 0) & (local >= 0) & (local < slab_tiles))
            def _():
                rows = pl.ds(pl.multiple_of(local * TILE, TILE), TILE)
                for c in range(block.shape[1] // TILE):
                    spot = cols_ref[index, c]

                    @pl.when(spot >= 0)
                    def _():
                        columns = pl.ds(pl.multiple_of(spot * TILE, TILE), TILE)
                        out_ref[rows, columns] += block[
                            r * TILE : (r + 1) * TILE, c * TILE : (c + 1) * TILE
                        ]


def update_front(row_places, col_places, parent, panels, arrived):
    height, width = parent.shape
    slab = min(SLAB, height)

    def kept(shape):
        return pl.BlockSpec(
            shape, lambda *_: (0,) * len(shape), pipeline_mode=pl.Buffered(1)
        )

    moving = pl.BlockSpec((slab, width), lambda i, *_: (i, 0))
    return pl.pallas_call(
        schur_kernel,
        out_shape=jax.ShapeDtypeStruct((height, width), jnp.float32),
        grid_spec=pltpu.PrefetchScalarGridSpec(
            num_scalar_prefetch=2,
            grid=(height // slab,),
            in_specs=[moving, kept(panels.shape)] + [kept(block.shape) for block in arrived],
            out_specs=moving,
            scratch_shapes=[pltpu.VMEM((width, 3 * PANEL), jnp.bfloat16)],
        ),
        compiler_params=pltpu.CompilerParams(vmem_limit_bytes=56 * 2**20),
        name="update_front",
    )(row_places, col_places, parent, panels, *arrived)


def on_device(child_pivot, child_border, child_update, parent_front, tile_map):
    subs = lax.axis_size("sub")
    columns = lax.axis_size("col")
    sub_index = lax.axis_index("sub")
    row_index = lax.axis_index("row")
    column_index = lax.axis_index("col")
    group = sub_index * columns + column_index
    border = child_border[0]
    update = child_update[0]
    child_rows, half_cols = update.shape
    group_width = half_cols // subs
    parent_rows, parent_cols = parent_front.shape
    row_tiles = child_rows // TILE
    group_tiles = group_width // TILE

    pivot = lax.all_gather(child_pivot[0], "row", axis=0, tiled=True)
    all_border = lax.all_gather(border, "row", axis=0, tiled=True)
    first_columns = jnp.where(group == 0, parent_front[:, :PANEL], 0.0)
    share = lax.psum_scatter(first_columns, ("sub", "col"), scatter_dimension=0, tiled=True)
    front_panel = lax.all_gather(share, ("row", "sub", "col"), axis=0, tiled=True)

    own_map = tile_map[sub_index]
    update_parts, border_parts = [], []
    for tile in range(PANEL // TILE):
        found = own_map == tile
        live = jnp.any(found)
        at = jnp.argmax(found).astype(jnp.int32) * TILE
        part = lax.dynamic_slice_in_dim(update, at, TILE, 1)
        update_parts.append(jnp.where(live & (column_index == 0), part, 0.0))
        part = lax.dynamic_slice_in_dim(all_border, at, TILE, 0)
        border_parts.append(jnp.where(live, part, 0.0))
    picked_update = lax.psum(jnp.concatenate(update_parts, axis=1), "col")
    picked_border = jnp.concatenate(border_parts, axis=0)

    inverse = invert_pivot(pivot)
    own_factor = times_transposed(border, inverse)
    picked_factor = times_transposed(picked_border, inverse)
    picked = picked_update - times_transposed(own_factor, picked_factor)
    sent = lax.all_gather(picked, ("sub", "row"), axis=0, tiled=True)
    sent = sent.reshape(subs, -1, PANEL)

    arrived, row_places, col_places = [], [], []
    for turn in range(subs):
        piece = lax.rem(sub_index + turn, subs)
        start = piece * group_width
        far = lax.dynamic_slice_in_dim(all_border, column_index * half_cols + start, group_width, 0)
        far_factor = times_transposed(far, inverse)
        contrib = lax.dynamic_slice_in_dim(update, start, group_width, 1)
        contrib = contrib - times_transposed(own_factor, far_factor)
        moves = [
            (s * columns + c, c * subs + (s + turn) % subs)
            for s in range(subs)
            for c in range(columns)
        ]
        arrived.append(lax.ppermute(contrib, ("sub", "col"), moves))
        child = lax.rem(lax.rem(group, subs) - turn + subs, subs)
        places = tile_map[child]
        rows = lax.dynamic_slice_in_dim(places, row_index * row_tiles, row_tiles, 0)
        cols = lax.dynamic_slice_in_dim(places, group * group_tiles, group_tiles, 0)
        row_places.append(jnp.where(rows < 0, -1, rows - row_index * (parent_rows // TILE)))
        col_places.append(jnp.where(cols < 0, -1, cols - group * (parent_cols // TILE)))

    top_inverse = invert_top(tile_map, front_panel, sent, parent_rows, child_rows)
    per_group = parent_cols // parent_rows
    block_ids = jnp.concatenate(
        [row_index[None], group * per_group + jnp.arange(per_group, dtype=jnp.int32)]
    ).astype(jnp.int32)
    panels = factor_panel(
        block_ids, tile_map, front_panel, sent, top_inverse, parent_rows, child_rows
    )
    schur_block = update_front(
        jnp.stack(row_places).astype(jnp.int32),
        jnp.stack(col_places).astype(jnp.int32),
        parent_front,
        panels,
        arrived,
    )
    return (schur_block, panels[:parent_rows])


def solution(mesh):
    placed = (
        P("sub", "row", None),
        P("sub", "row", None),
        P("sub", "row", "col"),
        P("row", ("sub", "col")),
        P(),
    )
    return jax.shard_map(
        on_device,
        mesh=mesh,
        in_specs=placed,
        out_specs=(P("row", ("sub", "col")), P("row", None)),
        check_vma=False,
    )
```

time: 1180 us -> 675 us (0.57); the launches traced: 1170 us -> 674 us
  other arithmetic: 363 us -> 10.9 us
  Pallas kernels: 0 us -> 238 us
  matrix products: 200 us -> 40.8 us
  local copies, waits for them, and re-layouts: 167 us -> 12 us
  waiting for transfers between devices: 409 us -> 351 us
    another operation x43 -> x4, other arithmetic: 310 us -> 2.39 us  [the longest x2 1.32 us: on_device(): at = jnp.argmax(found).astype(jnp.int32) * TILE]
    psum x3 -> x1, waiting for transfers between devices: 273 us -> 12 us  [on_device(): picked_update = lax.psum(jnp.concatenate(update_parts, axis=1), 'col')]
    pallas_call x0 -> x4, Pallas kernels: none -> 238 us  [the longest x1 157 us: invert_pivot(): pl.pallas_call(pivot_kernel, out_shape=jax.ShapeDtypeStruct((order, order...]
    all_gather x2 -> x4, waiting for transfers between devices: 76.4 us -> 311 us  [the longest x1 115 us: on_device(): sent = lax.all_gather(picked, ('sub', 'row'), axis=0, tiled=True)]
    another operation x49 -> x0, matrix products: 87.6 us -> none  [the longest x33 64 us: solve_rows(): jax.scipy.linalg.solve_triangular(lower_tri, right_rows.T, lower=True)]
    dot_general x4 -> x7, matrix products: 112 us -> 40.8 us  [times_transposed(): lax.dot_general(left, right, BY_COLUMNS, precision=high, preferred_elemen...]
    unnamed x24 -> x16, local copies, waits for them, and re-layouts: 74.6 us -> 8.94 us
    all_to_all x1 -> x0, waiting for transfers between devices: 59.3 us -> none  [on_device(): lax.all_to_all(padded, ('sub', 'col'), split_axis=1, concat_axis=0, tiled...]
  transfers between devices with their start and end apart: 6 -> 8, of which waited for: 5 -> 6; matrix products, arithmetic and copies ran while one was open for 32% -> 8% of each run, Pallas kernels for 0% -> 30%
where the time goes in v1:
time: 675 us; the launch traced here: 674 us
  waiting for transfers between devices  351 us (52%)
  Pallas kernels  238 us (35%)
  matrix products  40.8 us (6%)
  between operations  18.5 us (3%)
  local copies, waits for them, and re-layouts  12 us (2%)
  other arithmetic  10.9 us (2%)
    pallas_call x1, Pallas kernels, invert_pivot(): pl.pallas_call(pivot_kernel, out_shape=jax.ShapeDtypeStruct((order, order...  157 us
    all_gather x1, waiting for transfers between devices, on_device(): sent = lax.all_gather(picked, ('sub', 'row'), axis=0, tiled=True)  115 us
    all_gather x1, waiting for transfers between devices, on_device(): lax.all_gather(share, ('row', 'sub', 'col'), axis=0, tiled=True)  89.7 us
    all_gather x1, waiting for transfers between devices, on_device(): all_border = lax.all_gather(border, 'row', axis=0, tiled=True)  63.7 us
    all_gather x1, waiting for transfers between devices, on_device(): pivot = lax.all_gather(child_pivot[0], 'row', axis=0, tiled=True)  43 us
    dot_general x7, matrix products, times_transposed(): lax.dot_general(left, right, BY_COLUMNS, precision=high, preferred_elemen...  40.8 us
    pallas_call x1, Pallas kernels, invert_top(): pl.pallas_call(functools.partial(top_kernel, block_rows // TILE), out_sha...  35.8 us
    pallas_call x1, Pallas kernels, update_front(): pl.pallas_call(schur_kernel, out_shape=jax.ShapeDtypeStruct((height, widt...  34.8 us
  transfers between devices with their start and end apart: 8, of which 6 were waited for; matrix products, arithmetic and copies ran while one was open for 8% of the time, Pallas kernels for 30%

profile of v1, /device:TPU:0, one launch (start us, length us, event | category | flops | bytes accessed | tf_op | source)
XLA Modules:
  0.0 674.1 jit_solution(16464564135648294212)
XLA Ops:
  8.1 3.1 slice_select_fusion
  11.8 0.5 all-gather.13.cloned.1.call-update
  12.4 0.7 compare_reduce_fusion.1
  13.1 0.7 bitcast_reduce_fusion.1
  14.4 0.7 bitcast_reduce_fusion
  17.0 1.1 select_bitcast_fusion.3
  18.1 0.8 pad_maximum_fusion
  19.0 27.3 %reduce-scatter.2.cloned.1.call-done = f32[512,256]{1,0:T(8,128)} async-done(((f32[2048,256]{1,0:T(8,128)}), f32[512,256]{1,0:T(8,128)}) %reduce-scatter.2.cloned.1.call-update) | async-done | bytes 524304 | tf_op jit(solution)/shard_map/reduce_scatter | solution.py:281
  46.4 43.0 %all-gather.11.cloned.1.call-done = f32[1,1024,1024]{2,1,0:T(8,128)} async-done(((f32[1,128,1024]{2,1,0:T(8,128)}), f32[1,1024,1024]{2,1,0:T(8,128)}) %all-gather.11.cloned.1.call-update) | async-done | bytes 4194320 | tf_op jit(solution)/shard_map/all_gather | solution.py:278
  89.4 2.2 copy-done.4
  91.6 156.5 %invert_pivot.1 = f32[1024,1024]{1,0:T(8,128)S(1)} custom-call(f32[1024,1024]{1,0:T(8,128)S(1)} %bitcast.40), custom_call_target="tpu_custom_call" | custom-call | flops 42949672960 | bytes 8388608 | tf_op jit(solution)/shard_map/invert_pivot/pallas_call | solution.py:98
  248.1 2.0 copy-done.1
  250.1 3.7 fusion.6
  253.8 63.7 %all-gather.13.cloned.1.call-done = f32[1,4096,1024]{2,1,0:T(8,128)} async-done(((f32[1,512,1024]{2,1,0:T(8,128)}), f32[1,4096,1024]{2,1,0:T(8,128)}) %all-gather.13.cloned.1.call-update) | async-done | bytes 16777232 | tf_op jit(solution)/shard_map/all_gather | solution.py:279
  317.6 2.6 select_bitcast_fusion.1
  320.2 4.1 fusion.8
  324.3 12.0 %all-reduce.2.cloned.1.call-done = f32[512,256]{1,0:T(8,128)} async-done(((f32[512,256]{1,0:T(8,128)}), f32[512,256]{1,0:T(8,128)}) %all-reduce.2.cloned.1.call-update) | async-done | bytes 524304 | tf_op jit(solution)/shard_map/psum | solution.py:294
  336.3 2.9 convolution_subtract_fusion
  339.3 10.8 %fusion = f32[1024,1024]{1,0:T(8,128)S(1)} fusion(f32[1024,1024]{1,0:T(8,128)} %copy-done.1, f32[1,4096,1024]{2,1,0:T(8,128)} %all-gather.13.cloned.1.call-done, s32[]{:T(128)S(6)} %select_n.147), kind=kOutput, calls=%fused_computation | convolution fusion | flops 6442450944 | bytes 12582916 | tf_op jit(solution)/shard_map/dot_general | solution.py:25
  350.1 5.0 bitcast_subtract_fusion
  355.4 9.2 %fusion.2 = f32[1024,1024]{1,0:T(8,128)S(1)} fusion(f32[1024,1024]{1,0:T(8,128)S(1)} %copy-done.2, f32[1,4096,1024]{2,1,0:T(8,128)} %all-gather.13.cloned.1.call-done, s32[]{:T(128)S(6)} %select_n.145), kind=kOutput, calls=%fused_computation.2 | convolution fusion | flops 6442450944 | bytes 12582916 | tf_op jit(solution)/shard_map/dot_general | solution.py:25
  364.6 5.1 bitcast_subtract_fusion.1
  369.7 2.2 collective-permute-start
  372.1 0.5 pad_add_fusion.1.cols_ref
  373.2 89.7 %all-gather.7.cloned.1.call-done.front_ref = f32[16384,256]{1,0:T(8,128)} async-done(((f32[512,256]{1,0:T(8,128)}), f32[16384,256]{1,0:T(8,128)}) %all-gather.7.cloned.1.call-update) | async-done | bytes 16777232 | tf_op jit(solution)/shard_map/all_gather | solution.py:282
  462.9 114.5 %all-gather.9.cloned.1.call-done = f32[8192,256]{1,0:T(8,128)} async-done(((f32[512,256]{1,0:T(8,128)}), f32[8192,256]{1,0:T(8,128)}) %all-gather.9.cloned.1.call-update) | async-done | bytes 8388624 | tf_op jit(solution)/shard_map/all_gather | solution.py:301
  577.4 3.4 copy-done
  580.8 35.8 %invert_top.1.inverse_ref = f32[256,256]{1,0:T(8,128)S(1)} custom-call(s32[2,32]{1,0:T(2,128)S(1)} %copy-done.3, f32[16384,256]{1,0:T(8,128)} %all-gather.7.cloned.1.call-done.front_ref, f32[2,4096,256]{2,1,0:T(8,128)S(1)} %bitcast.39), custom_call_target="tpu_custom_call" | custom-call | tf_op jit(solution)/shard_map/invert_top/pallas_call | solution.py:133
  616.7 10.7 %factor_panel.1.panel_ref = f32[6144,256]{1,0:T(8,128)} custom-call(s32[3]{0:T(128)S(1)} %pad_add_fusion.2.ids_ref, s32[2,32]{1,0:T(2,128)S(1)} %copy-done.3, f32[16384,256]{1,0:T(8,128)} %all-gather.7.cloned.1.call-done.front_ref, f32[2,4096,256]{2,1,0:T(8,128)} %bitcast.38, f32[256,256]{1,0:T(8,128)S(1)} %invert_top.1.inverse_ref), custom_call_target="tpu_custom_call" | custom-call | tf_op jit(solution)/shard_map/factor_panel/pallas_call | solution.py:165
  627.4 3.0 slice.8
  630.4 1.3 copy-done.7
  631.8 34.8 %update_front.1 = f32[2048,4096]{1,0:T(8,128)} custom-call(s32[2,4]{1,0:T(2,128)} %pad_add_fusion.rows_ref, s32[2,8]{1,0:T(2,128)} %pad_add_fusion.1.cols_ref, f32[2048,4096]{1,0:T(8,128)} %parent_ref.1, f32[6144,256]{1,0:T(8,128)} %factor_panel.1.panel_ref, f32[512,1024]{1,0:T(8,128)} %copy-done.7, f32[512,1024]{1,0:T(8,128)} %collective-permute-done.1.rest_1_), custom_call_target="tpu_custom_call" | custom-call | tf_op jit(solution)/shard_map/update_front/pallas_call | solution.py:248
  (31 shorter events, 1.9 us)
Async XLA Ops:
  8.0 38.3 %reduce-scatter.2.cloned.1.call-start = ((), (), s32[]{:S(2)}) async-start(), calls=%async_computation.1 | async-start | bytes 2621440 | tf_op jit(solution)/shard_map/reduce_scatter | solution.py:281
  8.1 4.3 copy-start.3
  11.1 78.3 %all-gather.11.cloned.1.call-start = ((), (), s32[]{:S(2)}) async-start(), calls=%async_computation.5 | async-start | bytes 4718592 | tf_op jit(solution)/shard_map/all_gather | solution.py:278
  11.7 305.8 %all-gather.13.cloned.1.call-start = ((), (), s32[]{:S(2)}) async-start(), calls=%async_computation.6 | async-start | bytes 18874368 | tf_op jit(solution)/shard_map/all_gather | solution.py:279
  12.3 324.0 %all-reduce.2.cloned.1.call-start = ((), (), s32[]{:S(2)}) async-start(), calls=%async_computation.3 | async-start | bytes 1048576 | tf_op jit(solution)/shard_map/psum | solution.py:294
  19.0 443.9 %all-gather.7.cloned.1.call-start = ((), (), s32[]{:S(2)}) async-start(), calls=%async_computation.2 | async-start | bytes 17301504 | tf_op jit(solution)/shard_map/all_gather | solution.py:282
  46.3 531.1 %all-gather.9.cloned.1.call-start = ((), (), s32[]{:S(2)}) async-start(), calls=%async_computation.4 | async-start | bytes 8912896 | tf_op jit(solution)/shard_map/all_gather | solution.py:301
  89.4 2.2 copy-start.4
  91.6 158.5 %copy-start.5 = (f32[1,512,1024]{2,1,0:T(8,128)S(1)}, f32[1,512,1024]{2,1,0:T(8,128)}, u32[]{:S(2)}) copy-start(f32[1,512,1024]{2,1,0:T(8,128)} %param.6) | copy-start | bytes 6291460
  248.1 2.0 copy-start.1
  339.3 10.8 %copy-start.6 = (f32[1,512,2048]{2,1,0:T(8,128)S(1)}, f32[1,512,2048]{2,1,0:T(8,128)}, u32[]{:S(2)}) copy-start(f32[1,512,2048]{2,1,0:T(8,128)} %param.7) | copy-start | bytes 12582916
  350.1 5.3 copy-start.2
  355.1 275.3 %collective-permute-start.1 = (f32[512,1024]{1,0:T(8,128)}, f32[512,1024]{1,0:T(8,128)}, u32[]{:S(2)}, u32[]{:S(2)}) collective-permute-start(f32[512,1024]{1,0:T(8,128)} %bitcast_subtract_fusion), channel_id=1, source_target_pairs={{0,1},{1,17},{16,0},{17,16},{2,3},{3,19},{18,2},{19,18},{4,5},{5,2... | collective-permute-start | bytes 6291464 | tf_op jit(solution)/shard_map/ppermute | solution.py:317
  369.7 260.7 %collective-permute-start = (f32[512,1024]{1,0:T(8,128)}, f32[512,1024]{1,0:T(8,128)S(1)}, u32[]{:S(2)}, u32[]{:S(2)}) collective-permute-start(f32[512,1024]{1,0:T(8,128)} %bitcast_subtract_fusion.1), channel_id=1, source_target_pairs={{0,0},{1,16},{16,1},{17,17},{2,2},{3,18},{18,3},{19,19},{4,4},{5,2... | collective-permute-start | bytes 6291464 | tf_op jit(solution)/shard_map/ppermute | solution.py:317
  577.4 3.4 copy-start
  630.4 1.3 copy-start.7
Sparse Core Ops, SparseCore 0:
  12.1 34.1 reduce-scatter.1
Sparse Core Ops, SparseCore 1:
  13.7 75.6 all-gather.10
  91.4 226.1 all-gather.12
  319.8 16.5 all-reduce.1
  339.2 123.6 all-gather.6
  466.3 111.1 all-gather.8

commit v2 on v1

--- a/solution.py
+++ b/solution.py
@@ -37,8 +37,8 @@
         strip = rest[:STRIP]
         for step in range(STRIP):
             pivot = first + step
-            scale = lax.rsqrt(strip[step : step + 1, pivot : pivot + 1])
             column = jnp.broadcast_to(strip[:, pivot : pivot + 1], (STRIP, TILE))
+            scale = lax.rsqrt(column[step : step + 1])
             at_pivot = lane == pivot
             scaled = jnp.where(at_pivot[:1], 1.0, strip[step : step + 1]) * scale
             below = jnp.where(row > step, column, 0.0) * scale
@@ -84,7 +84,7 @@
     lax.fori_loop(0, tiles, eliminate, 0)
 
 
-def pivot_kernel(pivot_ref, inverse_ref, strip):
+def pivot_kernel(pivot_ref, first_ref, inverse_ref, strip):
     inverse_ref[...] = pivot_ref[...]
     invert_factor(inverse_ref, strip)
 
@@ -93,12 +93,12 @@
     return pl.BlockSpec(shape, lambda *_: (0,) * len(shape))
 
 
-def invert_pivot(pivot):
+def invert_pivot(pivot, first):
     order = pivot.shape[0]
     return pl.pallas_call(
         pivot_kernel,
         out_shape=jax.ShapeDtypeStruct((order, order), jnp.float32),
-        in_specs=[pl.BlockSpec(memory_space=pltpu.VMEM)],
+        in_specs=[pl.BlockSpec(memory_space=pltpu.VMEM), pl.BlockSpec(memory_space=pl.ANY)],
         out_specs=pl.BlockSpec(memory_space=pltpu.VMEM),
         scratch_shapes=[pltpu.VMEM((TILE, order), jnp.float32)],
         compiler_params=pltpu.CompilerParams(vmem_limit_bytes=40 * 2**20),
@@ -106,7 +106,7 @@
             flops=40 * order**3, bytes_accessed=8 * order**2, transcendentals=order
         ),
         name="invert_pivot",
-    )(pivot)
+    )(pivot, first)
 
 
 def add_row_tiles(map_ref, first, tiles, limit, sent_ref, target):
@@ -260,6 +260,38 @@
     )(row_places, col_places, parent, panels, *arrived)
 
 
+def half_pieces(border):
+    rows, columns = lax.axis_size("row"), lax.axis_size("col")
+    half = rows // columns
+    pieces = []
+    for turn in range(half):
+        moves = [
+            ((half * c + (i + turn) % half) * columns + i // half, i * columns + c)
+            for i in range(rows)
+            for c in range(columns)
+        ]
+        pieces.append(lax.ppermute(border, ("row", "col"), moves))
+    return pieces
+
+
+def in_order(pieces, row_index):
+    half = len(pieces)
+    height = pieces[0].shape[0]
+    result = jnp.zeros((half * height, pieces[0].shape[1]), pieces[0].dtype)
+    for turn, piece in enumerate(pieces):
+        place = lax.rem(row_index + turn, half) * height
+        result = lax.dynamic_update_slice_in_dim(result, piece, place, 0)
+    return result
+
+
+def from_first(block, share, column_index):
+    result = block if share is None else block[:share]
+    for c in range(1, lax.axis_size("col")):
+        piece = block if share is None else block[c * share : (c + 1) * share]
+        result = jnp.where(column_index == c, lax.ppermute(piece, "col", [(0, c)]), result)
+    return result
+
+
 def on_device(child_pivot, child_border, child_update, parent_front, tile_map):
     subs = lax.axis_size("sub")
     columns = lax.axis_size("col")
@@ -275,40 +307,53 @@
     row_tiles = child_rows // TILE
     group_tiles = group_width // TILE
 
-    pivot = lax.all_gather(child_pivot[0], "row", axis=0, tiled=True)
-    all_border = lax.all_gather(border, "row", axis=0, tiled=True)
+    pivot_rows = child_pivot.shape[1] // columns
+    pivot = lax.dynamic_slice_in_dim(child_pivot[0], column_index * pivot_rows, pivot_rows, 0)
+    pivot = lax.all_gather(pivot, ("row", "col"), axis=0, tiled=True)
+    far_border = half_pieces(border)
     first_columns = jnp.where(group == 0, parent_front[:, :PANEL], 0.0)
     share = lax.psum_scatter(first_columns, ("sub", "col"), scatter_dimension=0, tiled=True)
     front_panel = lax.all_gather(share, ("row", "sub", "col"), axis=0, tiled=True)
 
     own_map = tile_map[sub_index]
-    update_parts, border_parts = [], []
+    split = subs * lax.axis_size("row") * child_rows * PANEL <= parent_front.size
+    share_rows = child_rows // columns if split else child_rows
+    share_start = column_index * share_rows if split else 0
+    share_axes = ("sub", "row", "col") if split else ("sub", "row")
+    update_parts, spots = [], []
     for tile in range(PANEL // TILE):
         found = own_map == tile
         live = jnp.any(found)
         at = jnp.argmax(found).astype(jnp.int32) * TILE
         part = lax.dynamic_slice_in_dim(update, at, TILE, 1)
-        update_parts.append(jnp.where(live & (column_index == 0), part, 0.0))
-        part = lax.dynamic_slice_in_dim(all_border, at, TILE, 0)
-        border_parts.append(jnp.where(live, part, 0.0))
-    picked_update = lax.psum(jnp.concatenate(update_parts, axis=1), "col")
-    picked_border = jnp.concatenate(border_parts, axis=0)
-
-    inverse = invert_pivot(pivot)
+        update_parts.append(jnp.where(live, part, 0.0))
+        spots.append((live, at))
+    picked_update = from_first(jnp.concatenate(update_parts, axis=1), share_rows if split else None, column_index)
+
+    inverse = invert_pivot(pivot, share)
+    far_factor = in_order([times_transposed(piece, inverse) for piece in far_border], row_index)
     own_factor = times_transposed(border, inverse)
-    picked_factor = times_transposed(picked_border, inverse)
-    picked = picked_update - times_transposed(own_factor, picked_factor)
-    sent = lax.all_gather(picked, ("sub", "row"), axis=0, tiled=True)
+    picked_factor = jnp.concatenate(
+        [
+            jnp.where(live, lax.dynamic_slice_in_dim(far_factor, at, TILE, 0), 0.0)
+            for live, at in spots
+        ],
+        axis=0,
+    )
+    picked_factor = from_first(picked_factor, None, column_index)
+    share_factor = lax.dynamic_slice_in_dim(own_factor, share_start, share_rows, 0)
+    picked = picked_update - times_transposed(share_factor, picked_factor)
+    picked = jnp.where(front_panel[0, 0] > 0.0, picked, jnp.nan)
+    sent = lax.all_gather(picked, share_axes, axis=0, tiled=True)
     sent = sent.reshape(subs, -1, PANEL)
 
     arrived, row_places, col_places = [], [], []
     for turn in range(subs):
         piece = lax.rem(sub_index + turn, subs)
         start = piece * group_width
-        far = lax.dynamic_slice_in_dim(all_border, column_index * half_cols + start, group_width, 0)
-        far_factor = times_transposed(far, inverse)
+        far = lax.dynamic_slice_in_dim(far_factor, start, group_width, 0)
         contrib = lax.dynamic_slice_in_dim(update, start, group_width, 1)
-        contrib = contrib - times_transposed(own_factor, far_factor)
+        contrib = contrib - times_transposed(own_factor, far)
         moves = [
             (s * columns + c, c * subs + (s + turn) % subs)
             for s in range(subs)

time: 675 us -> 528 us (0.78)
  waiting for transfers between devices: 351 us -> 156 us
  starting transfers between devices: 2.71 us -> 83.8 us
  Pallas kernels: 238 us -> 184 us
  matrix products: 40.8 us -> 51.3 us
    all_gather x3 -> x2, waiting for transfers between devices: 221 us -> 122 us  [the longest x1 102 us: on_device(): sent = lax.all_gather(picked, share_axes, axis=0, tiled=True)]
    all_gather x1, waiting for transfers between devices: 89.7 us -> 0.03 us  [on_device(): lax.all_gather(share, ('row', 'sub', 'col'), axis=0, tiled=True)]
    ppermute x0 -> x6, starting transfers between devices: none -> 81.3 us  [the longest x2 75.9 us: from_first(): lax.ppermute(piece, 'col', [(0, c)])]
    pallas_call x1, Pallas kernels: 157 us -> 113 us  [invert_pivot(): pl.pallas_call(pivot_kernel, out_shape=jax.ShapeDtypeStruct((order, order...]
    psum x1 -> x0, waiting for transfers between devices: 12 us -> none  [on_device(): picked_update = lax.psum(jnp.concatenate(update_parts, axis=1), 'col')]
    pallas_call x1, Pallas kernels: 35.8 us -> 25.2 us  [invert_top(): pl.pallas_call(functools.partial(top_kernel, block_rows // TILE), out_sha...]
    dot_general x7 -> x8, matrix products: 40.8 us -> 51.3 us  [times_transposed(): lax.dot_general(left, right, BY_COLUMNS, precision=high, preferred_elemen...]
  transfers between devices with their start and end apart: 8 -> 12, of which waited for: 6 -> 3; matrix products, arithmetic and copies ran while one was open for 8% -> 12% of each run, Pallas kernels for 30% -> 29%
where the time goes in v2:
time: 528 us; the launch traced here: 523 us
  Pallas kernels  184 us (35%)
  waiting for transfers between devices  156 us (30%)
  starting transfers between devices  83.8 us (16%)
  matrix products  51.3 us (10%)
  local copies, waits for them, and re-layouts  18.2 us (3%)
  between operations  18.2 us (3%)
  other arithmetic  12.1 us (2%)
    pallas_call x1, Pallas kernels, invert_pivot(): pl.pallas_call(pivot_kernel, out_shape=jax.ShapeDtypeStruct((order, order...  113 us
    all_gather x1, waiting for transfers between devices, on_device(): sent = lax.all_gather(picked, share_axes, axis=0, tiled=True)  102 us
    ppermute x2, starting transfers between devices, from_first(): lax.ppermute(piece, 'col', [(0, c)])  75.9 us
    dot_general x8, matrix products, times_transposed(): lax.dot_general(left, right, BY_COLUMNS, precision=high, preferred_elemen...  51.3 us
    pallas_call x1, Pallas kernels, update_front(): pl.pallas_call(schur_kernel, out_shape=jax.ShapeDtypeStruct((height, widt...  34.9 us
    reduce_scatter x1, waiting for transfers between devices, on_device(): lax.psum_scatter(first_columns, ('sub', 'col'), scatter_dimension=0, tile...  34 us
    pallas_call x1, Pallas kernels, invert_top(): pl.pallas_call(functools.partial(top_kernel, block_rows // TILE), out_sha...  25.2 us
    all_gather x1, waiting for transfers between devices, on_device(): pivot = lax.all_gather(pivot, ('row', 'col'), axis=0, tiled=True)  19.9 us
  transfers between devices with their start and end apart: 12, of which 3 were waited for; matrix products, arithmetic and copies ran while one was open for 12% of the time, Pallas kernels for 29%

profile of v2, /device:TPU:0, one launch (start us, length us, event | category | flops | bytes accessed | tf_op | source)
XLA Modules:
  0.0 523.3 jit_solution(4925513757188512534)
XLA Ops:
  8.1 3.2 slice_select_fusion
  12.2 34.0 %reduce-scatter.2.cloned.1.call-done.first_ref = f32[512,256]{1,0:T(8,128)} async-done(((f32[2048,256]{1,0:T(8,128)}), f32[512,256]{1,0:T(8,128)}) %reduce-scatter.2.cloned.1.call-update) | async-done | bytes 524304 | tf_op jit(solution)/shard_map/reduce_scatter | solution.py:315
  46.3 2.0 collective-permute-start.1
  48.2 2.4 collective-permute-start.2
  55.0 19.9 %all-gather.9.cloned.1.call-done = f32[1,1024,1024]{2,1,0:T(8,128)} async-done(((f32[1,64,1024]{2,1,0:T(8,128)}), f32[1,1024,1024]{2,1,0:T(8,128)}) %all-gather.9.cloned.1.call-update) | async-done | bytes 4194320 | tf_op jit(solution)/shard_map/all_gather | solution.py:312
  74.9 1.0 copy-done.4
  75.9 2.2 copy-done.6
  78.1 113.3 %invert_pivot.1 = f32[1024,1024]{1,0:T(8,128)S(1)} custom-call(f32[1024,1024]{1,0:T(8,128)S(1)} %bitcast.40, f32[512,256]{1,0:T(8,128)S(1)} %copy-done.4), custom_call_target="tpu_custom_call" | custom-call | flops 42949672960 | bytes 8388608 | tf_op jit(solution)/shard_map/invert_pivot/pallas_call | solution.py:98
  191.5 1.1 broadcast_in_dim.39
  192.5 5.5 %bitcast_dynamic-update-slice_fusion.3 = f32[2048,1024]{1,0:T(8,128)S(1)} fusion(f32[2048,1024]{1,0:T(8,128)S(1)} %broadcast_in_dim.39, s32[]{:T(128)S(6)} %select_n.179, f32[1024,1024]{1,0:T(8,128)S(1)} %invert_pivot.1, f32[512,1024]{1,0:T(8,128)} %collective-permute-done.1), kind=kOutput, calls=%fused_computation.9 | convolution fusion | flops 3221225472 | bytes 8388612 | tf_op jit(solution)/shard_map/dot_general | solution.py:25
  198.1 5.1 bitcast_dynamic-update-slice_fusion.2
  203.2 5.1 bitcast_dynamic-update-slice_fusion.1
  208.3 5.3 %bitcast_dynamic-update-slice_fusion = f32[2048,1024]{1,0:T(8,128)S(1)} fusion(f32[2048,1024]{1,0:T(8,128)S(1)} %bitcast_dynamic-update-slice_fusion.1, s32[]{:T(128)S(6)} %select_n.182, f32[1024,1024]{1,0:T(8,128)S(1)} %invert_pivot.1, f32[512,1024]{1,0:T(8,128)} %collective-permute-done.4), kind=kOutput, calls=%fused_computation.6 | convolution fusion | flops 3221225472 | bytes 8388612 | tf_op jit(solution)/shard_map/dot_general | solution.py:25
  213.6 3.4 copy-done.7
  217.0 1.3 dynamic-slice_select_fusion.1
  218.3 1.1 pad_maximum_fusion
  219.4 73.9 %collective-permute-start.5 = (f32[256,1024]{1,0:T(8,128)}, f32[256,1024]{1,0:T(8,128)}, u32[]{:S(2)}, u32[]{:S(2)}) collective-permute-start(f32[256,1024]{1,0:T(8,128)} %pad_maximum_fusion), channel_id=1, source_target_pairs={{0,1},{2,3},{4,5},{6,7},{8,9},{10,11},{12,13},{14,15},{16,17},{18,... | collective-permute-start | bytes 3145736 | tf_op jit(solution)/shard_map/ppermute | solution.py:291
  293.3 2.4 select_bitcast_fusion
  297.0 2.0 collective-permute-start
  299.0 5.9 %fusion.23 = f32[1024,512]{1,0:T(8,128)S(1)} fusion(f32[1024,1024]{1,0:T(8,128)} %copy-done.2, f32[1,512,1024]{2,1,0:T(8,128)} %param.6), kind=kOutput, calls=%fused_computation.44 | convolution fusion | flops 3221225472 | bytes 8388608 | tf_op jit(solution)/shard_map/dot_general | solution.py:25
  305.0 1.3 slice.20
  307.0 2.7 fusion.15
  309.7 11.2 %bitcast_subtract_fusion = f32[512,1024]{1,0:T(8,128)} fusion(f32[1,512,2048]{2,1,0:T(8,128)} %param.7, s32[]{:T(128)S(6)} %select_n.189, f32[1024,512]{1,0:T(8,128)S(1)} %fusion.23, f32[2048,1024]{1,0:T(8,128)} %copy-done.7), kind=kOutput, calls=%fused_computation.4 | convolution fusion | flops 3221749760 | bytes 10486784 | tf_op jit(solution)/shard_map/dot_general | solution.py:25
  321.0 10.6 %bitcast_subtract_fusion.1 = f32[512,1024]{1,0:T(8,128)} fusion(f32[1,512,2048]{2,1,0:T(8,128)S(1)} %copy-done.8, s32[]{:T(128)S(6)} %select_n.188, f32[1024,512]{1,0:T(8,128)S(1)} %fusion.23, f32[2048,1024]{1,0:T(8,128)} %copy-done.7), kind=kOutput, calls=%fused_computation.5 | convolution fusion | flops 3221749760 | bytes 10486784 | tf_op jit(solution)/shard_map/dot_general | solution.py:25
  331.5 2.2 collective-permute-start.6
  335.2 101.7 %all-gather.7.cloned.1.call-done = f32[8192,256]{1,0:T(8,128)} async-done(((f32[256,256]{1,0:T(8,128)}), f32[8192,256]{1,0:T(8,128)}) %all-gather.7.cloned.1.call-update) | async-done | bytes 8388624 | tf_op jit(solution)/shard_map/all_gather | solution.py:347
  436.9 3.4 copy-done.3
  440.2 25.2 %invert_top.1.inverse_ref = f32[256,256]{1,0:T(8,128)S(1)} custom-call(s32[2,32]{1,0:T(2,128)S(1)} %copy-done.5, f32[16384,256]{1,0:T(8,128)} %all-gather.5.cloned.1.call-done.front_ref, f32[2,4096,256]{2,1,0:T(8,128)S(1)} %bitcast.39), custom_call_target="tpu_custom_call" | custom-call | tf_op jit(solution)/shard_map/invert_top/pallas_call | solution.py:133
  465.4 10.7 %factor_panel.1.panel_ref = f32[6144,256]{1,0:T(8,128)} custom-call(s32[3]{0:T(128)S(1)} %pad_add_fusion.2.ids_ref, s32[2,32]{1,0:T(2,128)S(1)} %copy-done.5, f32[16384,256]{1,0:T(8,128)} %all-gather.5.cloned.1.call-done.front_ref, f32[2,4096,256]{2,1,0:T(8,128)} %bitcast.38, f32[256,256]{1,0:T(8,128)S(1)} %invert_top.1.inverse_ref), custom_call_target="tpu_custom_call" | custom-call | tf_op jit(solution)/shard_map/factor_panel/pallas_call | solution.py:165
  476.1 3.0 slice.23
  479.2 1.4 copy-done.10
  480.5 34.9 %update_front.1 = f32[2048,4096]{1,0:T(8,128)} custom-call(s32[2,4]{1,0:T(2,128)} %pad_add_fusion.rows_ref, s32[2,8]{1,0:T(2,128)} %pad_add_fusion.1.cols_ref, f32[2048,4096]{1,0:T(8,128)} %parent_ref.1, f32[6144,256]{1,0:T(8,128)} %factor_panel.1.panel_ref, f32[512,1024]{1,0:T(8,128)} %copy-done.10, f32[512,1024]{1,0:T(8,128)} %collective-permute-done.7.rest_1_), custom_call_target="tpu_custom_call" | custom-call | tf_op jit(solution)/shard_map/update_front/pallas_call | solution.py:248
  (50 shorter events, 7.0 us)
Async XLA Ops:
  8.0 3.4 copy-start
  8.0 38.3 %copy-start.11 = (f32[1,512,1024]{2,1,0:T(8,128)S(1)}, f32[1,512,1024]{2,1,0:T(8,128)}, u32[]{:S(2)}) copy-start(f32[1,512,1024]{2,1,0:T(8,128)} %param.6) | copy-start | bytes 6291460
  8.0 43.7 %copy-start.5 = (s32[2,32]{1,0:T(2,128)S(1)}, s32[2,32]{1,0:T(2,128)}, u32[]{:S(2)}) copy-start(s32[2,32]{1,0:T(2,128)} %map_ref.3) | copy-start | bytes 772
  8.0 38.2 %reduce-scatter.2.cloned.1.call-start = ((), (), s32[]{:S(2)}) async-start(), calls=%async_computation.1 | async-start | bytes 2621440 | tf_op jit(solution)/shard_map/reduce_scatter | solution.py:315
  11.3 63.6 %all-gather.9.cloned.1.call-start = ((), (), s32[]{:S(2)}) async-start(), calls=%async_computation.4 | async-start | bytes 4456448 | tf_op jit(solution)/shard_map/all_gather | solution.py:312
  12.1 292.8 %all-gather.5.cloned.1.call-start = ((), (), s32[]{:S(2)}) async-start(), calls=%async_computation.2 | async-start | bytes 17301504 | tf_op jit(solution)/shard_map/all_gather | solution.py:316
  46.2 390.6 %all-gather.7.cloned.1.call-start = ((), (), s32[]{:S(2)}) async-start(), calls=%async_computation.3 | async-start | bytes 8650752 | tf_op jit(solution)/shard_map/all_gather | solution.py:347
  46.3 145.2 %collective-permute-start.1 = (f32[512,1024]{1,0:T(8,128)S(1)}, f32[512,1024]{1,0:T(8,128)}, u32[]{:S(2)}, u32[]{:S(2)}) collective-permute-start(f32[512,1024]{1,0:T(8,128)S(1)} %bitcast.41), channel_id=1, source_target_pairs={{0,0},{8,1},{2,2},{10,3},{4,4},{12,5},{6,6},{14,7},{1,8},{9,9},{3,... | collective-permute-start | bytes 6291464 | tf_op jit(solution)/shard_map/ppermute | solution.py:273
  48.2 149.8 %collective-permute-start.2 = (f32[512,1024]{1,0:T(8,128)S(1)}, f32[512,1024]{1,0:T(8,128)}, u32[]{:S(2)}, u32[]{:S(2)}) collective-permute-start(f32[512,1024]{1,0:T(8,128)S(1)} %bitcast.42), channel_id=1, source_target_pairs={{2,0},{10,1},{4,2},{12,3},{6,4},{14,5},{0,6},{8,7},{3,8},{11,9},{5... | collective-permute-start | bytes 6291464 | tf_op jit(solution)/shard_map/ppermute | solution.py:273
  50.6 152.5 %collective-permute-start.3 = (f32[512,1024]{1,0:T(8,128)S(1)}, f32[512,1024]{1,0:T(8,128)}, u32[]{:S(2)}, u32[]{:S(2)}) collective-permute-start(f32[512,1024]{1,0:T(8,128)S(1)} %bitcast.43), channel_id=1, source_target_pairs={{4,0},{12,1},{6,2},{14,3},{0,4},{8,5},{2,6},{10,7},{5,8},{13,9},{7... | collective-permute-start | bytes 6291464 | tf_op jit(solution)/shard_map/ppermute | solution.py:273
  51.2 157.1 %collective-permute-start.4 = (f32[512,1024]{1,0:T(8,128)S(1)}, f32[512,1024]{1,0:T(8,128)}, u32[]{:S(2)}, u32[]{:S(2)}) collective-permute-start(f32[512,1024]{1,0:T(8,128)S(1)} %bitcast.44), channel_id=1, source_target_pairs={{6,0},{14,1},{0,2},{8,3},{2,4},{10,5},{4,6},{12,7},{7,8},{15,9},{1... | collective-permute-start | bytes 6291464 | tf_op jit(solution)/shard_map/ppermute | solution.py:273
  74.9 1.0 copy-start.4
  75.9 2.2 copy-start.6
  191.5 16.8 %copy-start.2 = (f32[1024,1024]{1,0:T(8,128)}, f32[1024,1024]{1,0:T(8,128)S(1)}, u32[]{:S(2)}) copy-start(f32[1024,1024]{1,0:T(8,128)S(1)} %invert_pivot.1) | copy-start | bytes 12582916
  213.6 3.4 copy-start.7
  219.4 87.6 %collective-permute-start.5 = (f32[256,1024]{1,0:T(8,128)}, f32[256,1024]{1,0:T(8,128)}, u32[]{:S(2)}, u32[]{:S(2)}) collective-permute-start(f32[256,1024]{1,0:T(8,128)} %pad_maximum_fusion), channel_id=1, source_target_pairs={{0,1},{2,3},{4,5},{6,7},{8,9},{10,11},{12,13},{14,15},{16,17},{18,... | collective-permute-start | bytes 3145736 | tf_op jit(solution)/shard_map/ppermute | solution.py:291
  295.6 0.7 copy-start.9
  297.0 9.9 %collective-permute-start = (f32[256,256]{1,0:T(8,128)}, f32[256,256]{1,0:T(8,128)}, u32[]{:S(2)}, u32[]{:S(2)}) collective-permute-start(f32[256,256]{1,0:T(8,128)} %fusion.12), channel_id=1, source_target_pairs={{0,1},{2,3},{4,5},{6,7},{8,9},{10,11},{12,13},{14,15},{16,17},{18,... | collective-permute-start | bytes 786440 | tf_op jit(solution)/shard_map/ppermute | solution.py:291
  309.7 11.3 %copy-start.8 = (f32[1,512,2048]{2,1,0:T(8,128)S(1)}, f32[1,512,2048]{2,1,0:T(8,128)}, u32[]{:S(2)}) copy-start(f32[1,512,2048]{2,1,0:T(8,128)} %param.7) | copy-start | bytes 12582916
  321.0 158.2 %collective-permute-start.7 = (f32[512,1024]{1,0:T(8,128)}, f32[512,1024]{1,0:T(8,128)}, u32[]{:S(2)}, u32[]{:S(2)}) collective-permute-start(f32[512,1024]{1,0:T(8,128)} %bitcast_subtract_fusion), channel_id=1, source_target_pairs={{0,1},{1,17},{16,0},{17,16},{2,3},{3,19},{18,2},{19,18},{4,5},{5,2... | collective-permute-start | bytes 6291464 | tf_op jit(solution)/shard_map/ppermute | solution.py:362
  331.5 147.6 %collective-permute-start.6 = (f32[512,1024]{1,0:T(8,128)}, f32[512,1024]{1,0:T(8,128)S(1)}, u32[]{:S(2)}, u32[]{:S(2)}) collective-permute-start(f32[512,1024]{1,0:T(8,128)} %bitcast_subtract_fusion.1), channel_id=1, source_target_pairs={{0,0},{1,16},{16,1},{17,17},{2,2},{3,18},{18,3},{19,19},{4,4},{5,2... | collective-permute-start | bytes 6291464 | tf_op jit(solution)/shard_map/ppermute | solution.py:362
  436.9 3.4 copy-start.3
  479.2 1.4 copy-start.10
  480.5 34.9 %copy-start.1 = (f32[1,128,1024]{2,1,0:T(8,128)S(1)}, f32[1,128,1024]{2,1,0:T(8,128)}, u32[]{:S(2)}) copy-start(f32[1,128,1024]{2,1,0:T(8,128)} %param.5) | copy-start | bytes 1572868
Sparse Core Ops, SparseCore 0:
  12.0 34.1 reduce-scatter.1
Sparse Core Ops, SparseCore 1:
  14.5 60.3 all-gather.8
  78.0 209.5 all-gather.4
  309.8 127.0 all-gather.6
